TPU v7x, 128 devices: a whole 4x4x4 slice. The times are simulated.
128 devices in a mesh: owner: 32 (over z, y, core), rep: 4 (over x).
Axes of the slice: x: 4, y: 4, z: 4, core: 2. Of those that a mesh axis runs over, the one named last changes fastest.
Arguments:
- feat_codes: bfloat16 [65536, 768], P('owner'), may hold values from -1 to 1
- feat_scales: bfloat16 [65536], P('owner'), may hold values from 0.5 to 4
- hist_codes: bfloat16 [65536, 1024], P('owner'), may hold values from -1 to 1
- hist_scales: bfloat16 [65536], P('owner'), may hold values from 0.5 to 4
- batch_rows: int32 [32, 4, 512], P('owner'), may hold values from 0 to 2047, as said below
- send_rows: int32 [32, 4, 32, 32], P('owner', 'rep'), may hold values from 0 to 2047
- send_counts: int32 [32, 4, 32], P('owner', 'rep'), may hold values from 1 to 32, as said below
- block_ids: int32 [32, 4, 4, 8], P('owner', 'rep'), may hold values from 0 to 11
- block_counts: int32 [32, 4, 4], P('owner', 'rep'), may hold values from 1 to 8
- tiles: bfloat16 [32, 4, 4, 8, 128, 128], P('owner', 'rep'), may hold values from -0.1875 to 0.1875
- w_one: bfloat16 [1536, 1024], replicated, may hold values from -0.15625 to 0.15625
- w_two: bfloat16 [2048, 1024], replicated, may hold values from -0.125 to 0.125
- cotangent: bfloat16 [32, 4, 512, 1024], P('owner', 'rep'), may hold values from -0.0234375 to 0.0234375
Outputs:
- new_hist_codes: bfloat16 [65536, 1024], P('owner')
- new_hist_scales: bfloat16 [65536], P('owner')
- grad_one: float32 [1536, 1024], P('owner')
- grad_two: float32 [2048, 1024], P('owner')
Inputs may be any that keep to these rules, and one draw needn't show every extreme that they name: `batch_rows`: for each owner the rep groups' lists together hold every row of its shard exactly once. `send_rows`: entries at or past the matching send_counts are ignored. `send_counts`: in every rep group some batch receives 32 live rows from every owner. `block_ids`: entries at or past the matching block_counts are ignored; blocks may repeat.
All inputs are finite; a program needn't handle non-finite values.
Results may differ from a plain program's by a relative error of at most 0.013.
Values may be sent and summed in bfloat16 or wider, within the bound.
A program may use at most 128 MiB of HBM per device.

v0:
```python
import functools

import jax
import jax.numpy as jnp
from jax import lax
from jax.experimental import pallas as pl
from jax.experimental.pallas import tpu as pltpu
from jax.sharding import PartitionSpec as P

F = 768
H = 1024
B = 512
BLK = 128
KB = 8
QB = 4
NODE = 2048
NTAB = 12
MESH = pl.DeviceIdType.MESH
BF = jnp.bfloat16
F32 = jnp.float32

ROUNDS = (
    ((1, 0), (3, 0), (0, 1), (0, 3)),
    ((1, 1), (3, 3), (1, 3), (3, 1)),
    ((2, 0), (0, 2), (2, 2), (0, 0)),
    ((2, 1), (1, 2), (2, 3), (3, 2)),
)
PEERS = [(dz, dy, dc) for chips in ROUNDS for dc in (0, 1) for dz, dy in chips if (dz, dy, dc) != (0, 0, 0)]


def swish_slope(pre, sig):
    return sig * (1.0 + pre * (1.0 - sig))


def dot(left, right):
    return jnp.dot(left, right, preferred_element_type=F32)


def dot_rows(left, right):
    return lax.dot_general(left, right, (((0,), (0,)), ((), ())), preferred_element_type=F32)


def dot_cols(left, right):
    return lax.dot_general(left, right, (((1,), (1,)), ((), ())), preferred_element_type=F32)


def kernel(
    ids, brow, scales, idx_h, feat_h, hist_h, tiles_h, w1_h, w2_h, cot_h,
    hist_o, sc_o, g1_o, g2_o,
    table, w1, w2, tiles, cot, idxc, adj, sel, sendf, sendh, recvf, recvh,
    left1, left2, pre1, pre2, tmp, d2, back, d1, codes, scmsg, stage,
    part, r2, r1, pa, pb, pc, qa, qb, qc, pa2, pb2, pc2, qa2, qb2, qc2, pa3, pb3, pc3, gath,
    lsem, osem, fss, frs, hss, hrs, ass, ars, css, crs, rss, rrs,
):
    own = lax.axis_index("owner")
    x = lax.axis_index("rep")
    z = lax.div(own, 8)
    y = lax.rem(lax.div(own, 2), 4)
    c = lax.rem(own, 2)

    def at(dz, dy, dc, dx=0):
        zz, yy = lax.rem(z + dz, 4), lax.rem(y + dy, 4)
        return (zz * 8 + yy * 2 + lax.rem(c + dc, 2), lax.rem(x + dx, 4))

    def load(k, src, dst):
        cp = pltpu.make_async_copy(src, dst, lsem.at[k])
        cp.start()
        return cp

    def send(src, dst, ss, rs, k, dev):
        cp = pltpu.make_async_remote_copy(
            src_ref=src, dst_ref=dst, send_sem=ss.at[k], recv_sem=rs.at[k],
            device_id=dev, device_id_type=MESH,
        )
        cp.start()
        return cp

    ld_idx = load(0, idx_h, idxc)
    ld_feat = load(1, feat_h, table.at[:, pl.ds(0, F)])
    ld_tiles = load(2, tiles_h, tiles)
    ld_w1 = load(3, w1_h, w1)
    ld_w2 = load(4, w2_h, w2)
    ld_cot = load(5, cot_h, cot)

    bar = pltpu.get_barrier_semaphore()
    for dz, dy, dc in PEERS:
        pl.semaphore_signal(bar, inc=1, device_id=at(dz, dy, dc), device_id_type=MESH)
    for dx in (1, 2, 3):
        pl.semaphore_signal(bar, inc=1, device_id=at(0, 0, 0, dx), device_id_type=MESH)

    lane = lax.broadcasted_iota(jnp.int32, (64, 128), 1)

    def pick(starts, which):
        for i, start in enumerate(starts):
            col = idxc[pl.ds(pl.multiple_of(start, 64), 64), :]
            for t in range(NODE // 128):
                hit = col == lane + t * 128
                val = jnp.where(hit, scales[which : which + 1, t * 128 : (t + 1) * 128], 0.0)
                sel[i * 64 : (i + 1) * 64, t * 128 : (t + 1) * 128] = val.astype(BF)

    def halo(width, which, sendb, recvb, ss, rs, first):
        cps = []
        for chips in ROUNDS:
            nums = [lax.rem(z + dz, 4) * 4 + lax.rem(y + dy, 4) for dz, dy in chips]
            pick([n * 64 for n in nums], which)
            for t in range(width // 256):
                cols = slice(t * 256, (t + 1) * 256)
                res = dot(sel[...], table[:, cols]).astype(BF)
                for i, n in enumerate(nums):
                    sendb[n, :, cols] = res[i * 64 : (i + 1) * 64]
            if first:
                pl.semaphore_wait(bar, len(PEERS) + 3)
                first = False
            for dc in (0, 1):
                for n, (dz, dy) in zip(nums, chips):
                    cc = lax.rem(c + dc, 2)
                    src = sendb.at[n, pl.ds(pl.multiple_of(cc * 32, 32), 32)]
                    mine = pl.ds(pl.multiple_of(own * 32, 32), 32)
                    if (dz, dy, dc) == (0, 0, 0):
                        recvb[mine, :] = src[...]
                    else:
                        cps.append(send(src, recvb.at[mine], ss, rs, len(cps), at(dz, dy, dc)))
        return cps

    ld_idx.wait()
    ld_feat.wait()
    cps_f = halo(F, 0, sendf, recvf, fss, frs, True)
    for i in range(2):
        pick([1024 + x * B + i * 256 + j * 64 for j in range(4)], 0)
        for t in range(F // 256):
            cols = slice(t * 256, (t + 1) * 256)
            left1[i * 256 : (i + 1) * 256, cols] = dot(sel[...], table[:, cols]).astype(BF)
    ld_hist = load(6, hist_h, table)

    ld_tiles.wait()

    def fill(q, carry):
        rows = pl.ds(pl.multiple_of(q * BLK, BLK), BLK)
        for b in range(NTAB):
            acc = jnp.zeros((BLK, BLK), F32)
            for k in range(KB):
                acc += jnp.where(ids[q * KB + k] == b, tiles[q, k], jnp.zeros((), BF)).astype(F32)
            adj[rows, b * BLK : (b + 1) * BLK] = acc.astype(BF)
        return carry

    lax.fori_loop(0, QB, fill, 0)
    ld_hist.wait()
    cps_h = halo(H, 1, sendh, recvh, hss, hrs, False)

    ld_w1.wait()
    for i in range(2):
        rows = slice(i * 256, (i + 1) * 256)
        tmp[rows, :F] = dot(adj[rows, :B], left1[:, :F])
        pre1[rows, :] = dot(left1[rows, :F], w1[:F, :])
    for cp in cps_f:
        cp.wait_recv()
    ag = []
    for i in range(2):
        rows = slice(i * 256, (i + 1) * 256)
        left1[rows, F:] = (tmp[rows, :F] + dot(adj[rows, B:], recvf[...])).astype(BF)
        pre = pre1[rows, :] + dot(left1[rows, F:], w1[F:, :])
        sig = jax.nn.sigmoid(pre)
        hid = (pre * sig).astype(BF)
        pre1[rows, :] = swish_slope(pre, sig)
        left2[rows, :H] = hid
        wide = hid.astype(F32)
        scale = (jnp.max(jnp.abs(wide), axis=1, keepdims=True) + 1e-5).astype(BF).astype(F32)
        mine = pl.ds(pl.multiple_of(x * B + i * 256, 256), 256)
        codes[mine, :] = (wide * (1.0 / scale)).astype(BF)
        for j in range(2):
            turned = jnp.broadcast_to(scale[j * 128 : (j + 1) * 128], (128, 128)).T
            scmsg[x, 2 * i + j : 2 * i + j + 1, :] = turned[0:1]
        ag.append(send(codes.at[mine], codes.at[mine], ass, ars, 2 * i, at(0, 0, 0, 1)))
        ag.append(send(codes.at[mine], codes.at[mine], ass, ars, 2 * i + 1, at(0, 0, 0, 3)))
    for dx in (1, 2, 3):
        ag.append(send(scmsg.at[x], scmsg.at[x], ass, ars, 5 + dx, at(0, 0, 0, dx)))

    ld_w2.wait()
    ld_cot.wait()
    for i in range(2):
        rows = slice(i * 256, (i + 1) * 256)
        tmp[rows, :] = dot(adj[rows, :B], left2[:, :H])
        pre2[rows, :] = dot(left2[rows, :H], w2[:H, :])

    ag[0].wait_recv()
    far = pl.ds(pl.multiple_of(lax.rem(x + 3, 4) * B, B), 256)
    fwd = [send(codes.at[far], codes.at[far], ass, ars, 4, at(0, 0, 0, 1))]
    ag[3].wait_recv()
    far = pl.ds(pl.multiple_of(lax.rem(x + 1, 4) * B + 256, 256), 256)
    fwd.append(send(codes.at[far], codes.at[far], ass, ars, 5, at(0, 0, 0, 3)))

    for cp in cps_h:
        cp.wait_recv()
    for i in range(2):
        rows = slice(i * 256, (i + 1) * 256)
        left2[rows, H:] = (tmp[rows, :] + dot(adj[rows, B:], recvh[...])).astype(BF)
        pre = pre2[rows, :] + dot(left2[rows, H:], w2[H:, :])
        sig = jax.nn.sigmoid(pre)
        d2[rows, :] = (cot[rows, :].astype(F32) * swish_slope(pre, sig)).astype(BF)

    def term(left, delta, share, recv, base):
        width = 8 * share

        def one(zt, carry):
            cols = pl.ds(pl.multiple_of(zt * width, 128), width)
            lhs = left[:, cols]
            for t in range(4):
                res = dot_rows(lhs, delta[:, t * 256 : (t + 1) * 256]).astype(BF)
                for o in range(8):
                    part[zt, o // 2, o % 2, t, :share, :] = res[o * share : (o + 1) * share]
            pltpu.make_async_remote_copy(
                src_ref=part.at[zt, :, 1 - c, :, pl.ds(0, share)], dst_ref=recv.at[zt],
                send_sem=css.at[base + zt], recv_sem=crs.at[base + zt],
                device_id=at(0, 0, 1), device_id_type=MESH,
            ).start()
            return carry

        lax.fori_loop(0, 4, one, 0)

    def merge(share, recv, base):
        def one(zt, carry):
            cp = pltpu.make_async_remote_copy(
                src_ref=part.at[zt, :, 1 - c, :, pl.ds(0, share)], dst_ref=recv.at[zt],
                send_sem=css.at[base + zt], recv_sem=crs.at[base + zt],
                device_id=at(0, 0, 1), device_id_type=MESH,
            )
            cp.wait()
            for t in range(4):
                both = recv[zt, t].astype(F32) + part[zt, t, c, :, :share, :].astype(F32)
                recv[zt, t] = both.astype(BF)
            return carry

        lax.fori_loop(0, 4, one, 0)

    def others(k):
        return [(i, lax.rem(k + i + 1, 4)) for i in range(3)]

    def first_phase(recv, s, base, offs):
        (a0, an), (b0, bn), (c0, cn) = s
        oa, ob, oc = offs
        cps = []
        for i in range(3):
            yy, zz, xx = (lax.rem(k + i + 1, 4) for k in (y, z, x))
            cps.append(send(recv.at[:, yy, :, pl.ds(a0, an)], pa.at[i, :, :, pl.ds(oa, an)], rss, rrs, base + i, at(0, i + 1, 0)))
            cps.append(send(recv.at[zz, :, :, pl.ds(b0, bn)], pb.at[i, :, :, pl.ds(ob, bn)], rss, rrs, base + 3 + i, at(i + 1, 0, 0)))
            cps.append(send(recv.at[:, :, xx, pl.ds(c0, cn)], pc.at[i, :, :, pl.ds(oc, cn)], rss, rrs, base + 6 + i, at(0, 0, 0, i + 1)))
        return cps

    term(left2, d2, 64, r2, 0)
    for i in range(2):
        rows = slice(i * 256, (i + 1) * 256)
        back[rows, :] = dot_cols(d2[rows, :], w2[H:, :]).astype(BF)
    for i in range(2):
        rows = slice(i * 256, (i + 1) * 256)
        grad = dot_cols(d2[rows, :], w2[:H, :]) + dot_rows(adj[:, rows], back[...])
        d1[rows, :] = (grad * pre1[rows, :]).astype(BF)
    merge(64, r2, 0)
    p1 = first_phase(r2, ((0, 32), (32, 16), (48, 16)), 0, (0, 0, 0))
    term(left1, d1, 48, r1, 4)
    merge(48, r1, 4)
    p1 += first_phase(r1, ((0, 16), (16, 16), (32, 16)), 9, (32, 16, 16))

    for cp in [ag[1], ag[2]] + ag[4:] + fwd:
        cp.wait_recv()
    sub = lax.broadcasted_iota(jnp.int32, (256, 256), 0)

    def place(n, carry):
        for t in range(NODE // 256):
            cols = slice(t * 256, (t + 1) * 256)
            hit = sub + n * 256 == brow[0:1, cols]
            sel[:, cols] = jnp.where(hit, 1.0, 0.0).astype(BF)
        slot = lax.rem(n, 2)
        out = pltpu.make_async_copy(
            stage.at[slot], hist_o.at[pl.ds(pl.multiple_of(n * 256, 256), 256)], osem.at[slot]
        )

        @pl.when(n >= 2)
        def _():
            out.wait()

        for t in range(4):
            cols = slice(t * 256, (t + 1) * 256)
            stage[slot, :, cols] = dot(sel[...], codes[:, cols]).astype(BF)
        out.start()
        return carry

    lax.fori_loop(0, 8, place, 0)
    for slot in range(2):
        pltpu.make_async_copy(stage.at[slot], hist_o.at[pl.ds(0, 256)], osem.at[slot]).wait()

    sc_o[...] = jnp.zeros((8, NODE), F32)
    lane_w = lax.broadcasted_iota(jnp.int32, (128, 128), 1)

    def place_scale(k, carry):
        rr, j = lax.div(k, 4), lax.rem(k, 4)
        col = idxc[pl.ds(pl.multiple_of(1024 + k * 128, 128), 128), :]
        val = jnp.broadcast_to(scmsg[rr, pl.ds(j, 1), :], (128, 128)).T
        for t in range(NODE // 128):
            got = jnp.where(col == lane_w + t * 128, val, 0.0)
            sc_o[:, t * 128 : (t + 1) * 128] += jnp.sum(got.reshape(16, 8, 128), axis=0)
        return carry

    lax.fori_loop(0, 16, place_scale, 0)

    def wait(cps):
        for cp in cps:
            cp.wait_recv()

    def total(mine, got, *at_index):
        acc = mine.astype(F32)
        for i in range(3):
            acc += got[(i, *at_index)].astype(F32)
        return acc.astype(BF)

    wait(p1)

    def sum_one(k, carry):
        qa[k, :, 0:32] = total(r2[k, y, :, 0:32], pa, k, slice(None), slice(0, 32))
        qa[k, :, 32:48] = total(r1[k, y, :, 0:16], pa, k, slice(None), slice(32, 48))
        qb[k, :, 0:16] = total(r2[z, k, :, 32:48], pb, k, slice(None), slice(0, 16))
        qb[k, :, 16:32] = total(r1[z, k, :, 16:32], pb, k, slice(None), slice(16, 32))
        qc[k, :, 0:16] = total(r2[k, :, x, 48:64], pc, k, slice(None), slice(0, 16))
        qc[k, :, 16:32] = total(r1[k, :, x, 32:48], pc, k, slice(None), slice(16, 32))
        return carry

    lax.fori_loop(0, 4, sum_one, 0)
    p2 = []
    for i in range(3):
        yy, zz = lax.rem(y + i + 1, 4), lax.rem(z + i + 1, 4)
        p2.append(send(qa.at[zz], pa2.at[i], rss, rrs, 18 + i, at(i + 1, 0, 0)))
        p2.append(send(qb.at[yy], pb2.at[i], rss, rrs, 21 + i, at(0, i + 1, 0)))
        p2.append(send(qc.at[:, yy], pc2.at[i], rss, rrs, 24 + i, at(0, i + 1, 0)))
    wait(p2)

    def sum_two(k, carry):
        qa2[k] = total(qa[z, k], pa2, k)
        qb2[k] = total(qb[y, k], pb2, k)
        qc2[k] = total(qc[k, y], pc2, k)
        return carry

    lax.fori_loop(0, 4, sum_two, 0)
    p3 = []
    for i in range(3):
        xx, zz = lax.rem(x + i + 1, 4), lax.rem(z + i + 1, 4)
        p3.append(send(qa2.at[xx], pa3.at[i], rss, rrs, 27 + i, at(0, 0, 0, i + 1)))
        p3.append(send(qb2.at[xx], pb3.at[i], rss, rrs, 30 + i, at(0, 0, 0, i + 1)))
        p3.append(send(qc2.at[zz], pc3.at[i], rss, rrs, 33 + i, at(i + 1, 0, 0)))
    wait(p3)
    gath[x, 0:48] = total(qa2[x], pa3)
    gath[x, 48:80] = total(qb2[x], pb3)
    gath[x, 80:112] = total(qc2[z], pc3)
    p4 = [send(gath.at[x], gath.at[x], rss, rrs, 36 + i, at(0, 0, 0, i + 1)) for i in range(3)]
    wait(p4)
    for t in range(4):
        cols = slice(t * 256, (t + 1) * 256)
        got = gath[t].astype(F32)
        g2_o[0:32, cols] = got[0:32]
        g1_o[0:16, cols] = got[32:48]
        g2_o[32:48, cols] = got[48:64]
        g1_o[16:32, cols] = got[64:80]
        g2_o[48:64, cols] = got[80:96]
        g1_o[32:48, cols] = got[96:112]
    for cp in cps_f + cps_h + ag + fwd + p1 + p2 + p3 + p4:
        cp.wait_send()


def shards(feat_codes, feat_scales, hist_codes, hist_scales, batch_rows, send_rows, send_counts,
           block_ids, block_counts, tiles, w_one, w_two, cotangent):
    live = jnp.arange(32)[None, :] < send_counts[0, 0][:, None]
    picks = jnp.where(live, send_rows[0, 0], -1).reshape(-1)
    placed = batch_rows[0].reshape(-1)
    idx = jnp.broadcast_to(jnp.concatenate([picks, placed])[:, None], (3072, 128))
    ids = jnp.where(jnp.arange(KB)[None, :] < block_counts[0, 0][:, None], block_ids[0, 0], -1).reshape(-1)
    scales = jnp.stack([feat_scales, hist_scales]).astype(F32)
    hbm = pl.BlockSpec(memory_space=pl.ANY)
    vmem = pl.BlockSpec(memory_space=pltpu.VMEM)
    smem = pl.BlockSpec(memory_space=pltpu.SMEM)
    v = pltpu.VMEM
    dma = pltpu.SemaphoreType.DMA
    scratch = [
        v((NODE, H), BF), v((2 * F, H), BF), v((2 * H, H), BF), v((QB, KB, BLK, BLK), BF), v((B, H), BF),
        v((3072, 128), jnp.int32), v((B, NTAB * BLK), BF), v((256, NODE), BF),
        v((16, 64, F), BF), v((16, 64, H), BF), v((1024, F), BF), v((1024, H), BF),
        v((B, 2 * F), BF), v((B, 2 * H), BF), v((B, H), F32), v((B, H), F32), v((B, H), F32),
        v((B, H), BF), v((B, H), BF), v((B, H), BF), v((4 * B, H), BF), v((4, 8, 128), F32),
        v((2, 256, H), BF),
        v((4, 4, 2, 4, 64, 256), BF), v((4, 4, 4, 64, 256), BF), v((4, 4, 4, 48, 256), BF),
        v((3, 4, 4, 48, 256), BF), v((3, 4, 4, 32, 256), BF), v((3, 4, 4, 32, 256), BF),
        v((4, 4, 48, 256), BF), v((4, 4, 32, 256), BF), v((4, 4, 32, 256), BF),
        v((3, 4, 48, 256), BF), v((3, 4, 32, 256), BF), v((3, 4, 32, 256), BF),
        v((4, 48, 256), BF), v((4, 32, 256), BF), v((4, 32, 256), BF),
        v((3, 48, 256), BF), v((3, 32, 256), BF), v((3, 32, 256), BF),
        v((4, 112, 256), BF),
        dma((7,)), dma((2,)), dma((31,)), dma((31,)), dma((31,)), dma((31,)),
        dma((9,)), dma((9,)), dma((8,)), dma((8,)), dma((39,)), dma((39,)),
    ]
    hist_out, sc, g1, g2 = pl.pallas_call(
        kernel,
        out_shape=(
            jax.ShapeDtypeStruct((NODE, H), BF),
            jax.ShapeDtypeStruct((8, NODE), F32),
            jax.ShapeDtypeStruct((48, H), F32),
            jax.ShapeDtypeStruct((64, H), F32),
        ),
        in_specs=[smem, vmem, vmem] + [hbm] * 7,
        out_specs=(hbm, vmem, vmem, vmem),
        scratch_shapes=scratch,
        compiler_params=pltpu.CompilerParams(
            collective_id=0, has_side_effects=True, vmem_limit_bytes=62 << 20
        ),
        cost_estimate=pl.CostEstimate(flops=30_000_000_000, bytes_accessed=30_000_000, transcendentals=1_000_000),
    )(
        ids, placed[None, :], scales, idx, feat_codes, hist_codes, tiles[0, 0], w_one, w_two, cotangent[0, 0]
    )
    return hist_out, jnp.sum(sc, axis=0).astype(BF), g1, g2


def solution(mesh):
    in_specs = (
        P("owner", None), P("owner"), P("owner", None), P("owner"), P("owner", None, None),
        P("owner", "rep", None, None), P("owner", "rep", None), P("owner", "rep", None, None),
        P("owner", "rep", None), P("owner", "rep", None, None, None, None), P(), P(),
        P("owner", "rep", None, None),
    )
    out_specs = (P("owner", None), P("owner"), P("owner", None), P("owner", None))
    return jax.shard_map(shards, mesh=mesh, in_specs=in_specs, out_specs=out_specs, check_vma=False)
```

profile of v0, /device:TPU:0, one launch (start us, length us, event | category | flops | bytes accessed | tf_op | source)
XLA Modules:
  0.0 124.5 jit_solution(17149692076393216729)
XLA Ops:
  0.6 0.8 squeeze.12
  1.4 0.7 iota_compare_fusion.1
  2.1 0.1 lt.42
  2.2 0.5 broadcast_select_fusion.1.ids
  2.7 0.8 squeeze.13
  3.5 0.7 iota_compare_fusion
  4.2 0.1 lt.47
  4.3 0.7 stack.9
  5.0 0.7 stack.10
  5.7 0.6 maximum_convert_fusion.scales
  6.4 1.3 %copy.17 = s32[1,1,4,512]{3,1,2,0:T(1,128)} copy(s32[1,1,4,512]{3,2,1,0:T(4,128)} %bitcast.11) | data formatting | bytes 16384
  7.7 0.7 copy.18
  8.4 2.2 %broadcast_in_dim.18.idx_h = s32[3072,128]{1,0:T(8,128)} broadcast(s32[3072]{0:T(1024)S(1)} %pad_add_fusion), dimensions={0} | broadcast | bytes 1585152 | tf_op jit(solution)/shard_map/broadcast_in_dim | solution.py:372
  10.6 106.3 %shard_map.156 = (bf16[2048,1024]{1,0:T(8,128)(2,1)}, f32[8,2048]{1,0:T(8,128)}, f32[48,1024]{1,0:T(8,128)}, f32[64,1024]{1,0:T(8,128)}) custom-call(s32[32]{0:T(128)} %broadcast_select_fusion.1.ids, s32[1,2048]{1,0:T(1,128)} %bitcast.13, f32[2,2048]{1,0:T(2,128)} %maximum_convert_fusion.scales, s32[3072,128]{1,0:T(8,128)} %broadcast_in_dim.18.idx_h, ...), custom_call_target="tpu_custom_call" | custom-call | flops 30000001024 | bytes 30000000 | tf_op jit(solution)/shard_map/pallas_call | solution.py:397
  116.9 1.5 %reduce_sum.9 = bf16[2048]{0:T(1024)(128)(2,1)} reduce(f32[8,2048]{1,0:T(8,128)} %get-tuple-element.9, f32[]{:T(128)} %constant.1.clone.1), dimensions={0}, to_apply=%region_0.1 | reduce | flops 14336 | bytes 69636 | tf_op jit(solution)/shard_map/reduce_sum | solution.py:415
  118.4 0.0 copy-start.1
  118.4 0.0 copy-start
  118.4 4.7 %copy.22 = bf16[2048,1024]{1,0:T(8,128)(2,1)} copy(bf16[2048,1024]{1,0:T(8,128)(2,1)} %get-tuple-element.16) | data formatting | bytes 8388608
  123.1 0.0 copy-done.1
  123.1 0.7 copy.23
  123.8 0.0 copy-done
  123.8 0.7 copy.24
  (2 shorter events, 0.0 us)
Async XLA Ops:
  118.4 4.7 %copy-start.1 = (f32[48,1024]{1,0:T(8,128)S(1)}, f32[48,1024]{1,0:T(8,128)}, u32[]{:S(2)}) copy-start(f32[48,1024]{1,0:T(8,128)} %get-tuple-element.18) | copy-start | bytes 589828
  118.4 5.4 %copy-start = (f32[64,1024]{1,0:T(8,128)S(1)}, f32[64,1024]{1,0:T(8,128)}, u32[]{:S(2)}) copy-start(f32[64,1024]{1,0:T(8,128)} %get-tuple-element.19) | copy-start | bytes 786436
where the time goes:
time: 125 us; the launch traced here: 124 us
  Pallas kernels  106 us (85%)
  local copies, waits for them, and re-layouts  13.4 us (11%)
  other arithmetic  4.07 us (3%)
    pallas_call x1, Pallas kernels, shards(): pl.pallas_call(kernel, out_shape=(jax.ShapeDtypeStruct((NODE, H), BF), ja...  106 us
    unnamed x9, local copies, waits for them, and re-layouts  8.08 us

commit v1 on v0

v1 whole, which is shorter than its diff:
```python
import functools

import jax
import jax.numpy as jnp
from jax import lax
from jax.experimental import pallas as pl
from jax.experimental.pallas import tpu as pltpu
from jax.sharding import PartitionSpec as P

F = 768
H = 1024
B = 512
BLK = 128
KB = 8
QB = 4
NODE = 2048
NTAB = 12
MESH = pl.DeviceIdType.MESH
BF = jnp.bfloat16
F32 = jnp.float32

ROUNDS = (
    ((1, 0), (3, 0), (0, 1), (0, 3)),
    ((1, 1), (3, 3), (1, 3), (3, 1)),
    ((2, 0), (0, 2), (2, 2), (0, 0)),
    ((2, 1), (1, 2), (2, 3), (3, 2)),
)
PEERS = [(dz, dy, dc) for chips in ROUNDS for dc in (0, 1) for dz, dy in chips if (dz, dy, dc) != (0, 0, 0)]


def swish_slope(pre, sig):
    return sig * (1.0 + pre * (1.0 - sig))


def dot(left, right):
    return jnp.dot(left, right, preferred_element_type=F32)


def dot_rows(left, right):
    return lax.dot_general(left, right, (((0,), (0,)), ((), ())), preferred_element_type=F32)


def dot_cols(left, right):
    return lax.dot_general(left, right, (((1,), (1,)), ((), ())), preferred_element_type=F32)


def kernel(
    ids, counts, brow_h, srow_h, scount_h, fscale_h, hscale_h, feat_h, hist_h, tiles_h, w1_h, w2_h, cot_h,
    hist_o, sc_o, two_o, one_o,
    brow, srow, scount, fscale, hscale, sc,
    table, w1, w2, tiles, cot, idxc, adj, adjt, sel, sendf, sendh, recvf, recvh,
    left1, left2, pre1, pre2, tmp, d2, d1, codes, scmsg, stage, part,
    r2, pa2, pb2, pc2, qa2, qb2, qc2, ra2, rb2, rc2, g2,
    r1, pa1, pb1, pc1, qa1, qb1, qc1, ra1, rb1, rc1, g1,
    lsem, osem, fss, frs, hss, hrs, ass, ars, css, crs, rss, rrs,
):
    own = lax.axis_index("owner")
    x = lax.axis_index("rep")
    z = lax.div(own, 8)
    y = lax.rem(lax.div(own, 2), 4)
    c = lax.rem(own, 2)

    def at(dz, dy, dc, dx=0):
        zz, yy = lax.rem(z + dz, 4), lax.rem(y + dy, 4)
        return (zz * 8 + yy * 2 + lax.rem(c + dc, 2), lax.rem(x + dx, 4))

    def load(k, src, dst):
        cp = pltpu.make_async_copy(src, dst, lsem.at[k])
        cp.start()
        return cp

    def send(src, dst, ss, rs, k, dev):
        cp = pltpu.make_async_remote_copy(
            src_ref=src, dst_ref=dst, send_sem=ss.at[k], recv_sem=rs.at[k],
            device_id=dev, device_id_type=MESH,
        )
        cp.start()
        return cp

    bar = pltpu.get_barrier_semaphore()
    for dz, dy, dc in PEERS:
        pl.semaphore_signal(bar, inc=1, device_id=at(dz, dy, dc), device_id_type=MESH)
    for dx in (1, 2, 3):
        pl.semaphore_signal(bar, inc=1, device_id=at(0, 0, 0, dx), device_id_type=MESH)

    smalls = [
        load(7 + i, src, dst)
        for i, (src, dst) in enumerate(
            ((scount_h, scount), (srow_h, srow), (brow_h, brow), (fscale_h, fscale), (hscale_h, hscale))
        )
    ]
    ld_feat = load(1, feat_h, table.at[:, pl.ds(0, F)])
    ld_tiles = load(2, tiles_h, tiles)
    ld_w1 = load(3, w1_h, w1)
    ld_w2 = load(4, w2_h, w2)
    ld_cot = load(5, cot_h, cot)
    for cp in smalls:
        cp.wait()

    alive = lax.broadcasted_iota(jnp.int32, (32, 32), 0) < scount[0]
    turned = jnp.where(alive, srow[0, 0].T, -1)
    for d in range(32):
        idxc[d * 32 : (d + 1) * 32, :] = jnp.broadcast_to(turned[:, d : d + 1], (32, 128))

    def spread(k, carry):
        line = brow[0, pl.ds(k, 1), :]
        for j in range(4):
            wide = jnp.broadcast_to(line[:, j * 128 : (j + 1) * 128], (128, 128)).T
            idxc[pl.ds(pl.multiple_of(1024 + k * B + j * 128, 128), 128), :] = wide
        return carry

    lax.fori_loop(0, 4, spread, 0)
    scales = (fscale[...].astype(F32).reshape(1, NODE), hscale[...].astype(F32).reshape(1, NODE))

    lane = lax.broadcasted_iota(jnp.int32, (64, 128), 1)

    def pick(starts, which):
        for i, start in enumerate(starts):
            col = idxc[pl.ds(pl.multiple_of(start, 64), 64), :]
            for t in range(NODE // 128):
                hit = col == lane + t * 128
                val = jnp.where(hit, scales[which][:, t * 128 : (t + 1) * 128], 0.0)
                sel[i * 64 : (i + 1) * 64, t * 128 : (t + 1) * 128] = val.astype(BF)

    def halo(chips, width, which, sendb, recvb, ss, rs, first, gate):
        cps = []
        nums = [lax.rem(z + dz, 4) * 4 + lax.rem(y + dy, 4) for dz, dy in chips]
        pick([n * 64 for n in nums], which)
        for t in range(width // 256):
            cols = slice(t * 256, (t + 1) * 256)
            res = dot(sel[...], table[:, cols]).astype(BF)
            for i, n in enumerate(nums):
                sendb[n, :, cols] = res[i * 64 : (i + 1) * 64]
        if first == 0 and width == F:
            pl.semaphore_wait(bar, len(PEERS) + 3)
        for cp in gate:
            cp.wait_send()
        for dc in (0, 1):
            for n, (dz, dy) in zip(nums, chips):
                cc = lax.rem(c + dc, 2)
                src = sendb.at[n, pl.ds(pl.multiple_of(cc * 32, 32), 32)]
                mine = pl.ds(pl.multiple_of(own * 32, 32), 32)
                if (dz, dy, dc) == (0, 0, 0):
                    recvb[mine, :] = src[...]
                else:
                    cps.append(send(src, recvb.at[mine], ss, rs, first + len(cps), at(dz, dy, dc)))
        return cps

    ld_feat.wait()
    cps_f = []
    for chips in ROUNDS:
        cps_f += halo(chips, F, 0, sendf, recvf, fss, frs, len(cps_f), [])
    for i in range(2):
        pick([1024 + x * B + i * 256 + j * 64 for j in range(4)], 0)
        for t in range(F // 256):
            cols = slice(t * 256, (t + 1) * 256)
            left1[i * 256 : (i + 1) * 256, cols] = dot(sel[...], table[:, cols]).astype(BF)
    ld_hist = load(6, hist_h, table)

    ld_tiles.wait()

    def fill(q, carry):
        rows = pl.ds(pl.multiple_of(q * BLK, BLK), BLK)
        for b in range(NTAB):
            acc = jnp.zeros((BLK, BLK), F32)
            for k in range(KB):
                acc += jnp.where((ids[0, 0, q, k] == b) & (k < counts[0, 0, q]), tiles[q, k], jnp.zeros((), BF)).astype(F32)
            adj[rows, b * BLK : (b + 1) * BLK] = acc.astype(BF)
        return carry

    lax.fori_loop(0, QB, fill, 0)
    adjt[...] = adj[:, :B].T
    ld_hist.wait()
    cps_h = []
    for chips, (k0, k1) in zip(ROUNDS[:3], ((0, 16), (16, 23), (23, 31))):
        cps_h += halo(chips, H, 1, sendh, recvh, hss, hrs, len(cps_h), cps_f[k0:k1])

    ld_w1.wait()
    for t in range(F // 256):
        cols = slice(t * 256, (t + 1) * 256)
        tmp[:, cols] = dot(adj[:, :B], left1[:, cols])
    for t in range(4):
        cols = slice(t * 256, (t + 1) * 256)
        pre1[:, cols] = dot(left1[:, :F], w1[:F, cols])
    for cp in cps_f:
        cp.wait_recv()
    ag = []
    for i in range(2):
        rows = slice(i * 256, (i + 1) * 256)
        left1[rows, F:] = (tmp[rows, :F] + dot(adj[rows, B:], recvf[...])).astype(BF)
        pre = pre1[rows, :] + dot(left1[rows, F:], w1[F:, :])
        sig = jax.nn.sigmoid(pre)
        hid = (pre * sig).astype(BF)
        pre1[rows, :] = swish_slope(pre, sig)
        left2[rows, :H] = hid
        wide = hid.astype(F32)
        scale = (jnp.max(jnp.abs(wide), axis=1, keepdims=True) + 1e-5).astype(BF).astype(F32)
        mine = pl.ds(pl.multiple_of(x * B + i * 256, 256), 256)
        codes[mine, :] = (wide * (1.0 / scale)).astype(BF)
        for j in range(2):
            wide = jnp.broadcast_to(scale[j * 128 : (j + 1) * 128], (128, 128)).T
            scmsg[x, 2 * i + j : 2 * i + j + 1, :] = wide[0:1]
        ag.append(send(codes.at[mine], codes.at[mine], ass, ars, i, at(0, 0, 0, 1)))
    for i in (1, 0):
        mine = pl.ds(pl.multiple_of(x * B + i * 256, 256), 256)
        ag.append(send(codes.at[mine], codes.at[mine], ass, ars, 2 + i, at(0, 0, 0, 3)))
    for dx in (1, 2, 3):
        ag.append(send(scmsg.at[x], scmsg.at[x], ass, ars, 5 + dx, at(0, 0, 0, dx)))

    cps_h += halo(ROUNDS[3], H, 1, sendh, recvh, hss, hrs, len(cps_h), [])

    ld_w2.wait()
    ld_cot.wait()
    for t in range(4):
        cols = slice(t * 256, (t + 1) * 256)
        tmp[:, cols] = dot(adj[:, :B], left2[:, cols])
        pre2[:, cols] = dot(left2[:, :H], w2[:H, cols])
        table[cols, :B] = left2[:, cols].T
    for t in range(6):
        cols = slice(t * 256, (t + 1) * 256)
        table[cols, B:] = left1[:, cols].T

    ag[0].wait_recv()
    far = pl.ds(pl.multiple_of(lax.rem(x + 3, 4) * B, B), 256)
    fwd = [send(codes.at[far], codes.at[far], ass, ars, 4, at(0, 0, 0, 1))]
    ag[2].wait_recv()
    far = pl.ds(pl.multiple_of(lax.rem(x + 1, 4) * B + 256, 256), 256)
    fwd.append(send(codes.at[far], codes.at[far], ass, ars, 5, at(0, 0, 0, 3)))

    for cp in cps_h:
        cp.wait_recv()
    for t in range(4):
        cols = slice(t * 256, (t + 1) * 256)
        agg = (tmp[:, cols] + dot(adj[:, B:], recvh[:, cols])).astype(BF)
        left2[:, H + t * 256 : H + (t + 1) * 256] = agg
        table[H + t * 256 : H + (t + 1) * 256, :B] = agg.T
    for t in range(4):
        cols = slice(t * 256, (t + 1) * 256)
        pre = pre2[:, cols] + dot(left2[:, H:], w2[H:, cols])
        sig = jax.nn.sigmoid(pre)
        d2[:, cols] = (cot[:, cols].astype(F32) * swish_slope(pre, sig)).astype(BF)

    def swap(zt, subs, recv, base):
        return pltpu.make_async_remote_copy(
            src_ref=part.at[zt, :, 1 - c, :, pl.ds(0, subs)], dst_ref=recv.at[zt],
            send_sem=css.at[base], recv_sem=crs.at[base],
            device_id=at(0, 0, 1), device_id_type=MESH,
        )

    def piece(i, lanes, delta, share, recv, base):
        zt = lax.rem(z + i + 1, 4)
        lhs = table[pl.ds(pl.multiple_of(zt * 8 * share, 128), 8 * share), lanes]
        for t in range(4):
            res = dot(lhs, delta[:, t * 256 : (t + 1) * 256]).astype(BF)
            for o in range(8):
                for k in range(share // 8):
                    r0, c0 = o * share + k // 2 * 16, k % 2 * 128
                    part[zt, o // 2, o % 2, t, k] = res[r0 : r0 + 16, c0 : c0 + 128]
        swap(zt, share // 8, recv, base + i).start()

    def merge(i, subs, recv, base):
        zt = lax.rem(z + i + 1, 4)
        swap(zt, subs, recv, base + i).wait()
        for t in range(4):
            both = recv[zt, t].astype(F32) + part[zt, t, c, :, :subs].astype(F32)
            recv[zt, t] = both.astype(BF)

    def wait(cps):
        for cp in cps:
            cp.wait_recv()

    def total(mine, got, *at_index):
        acc = mine.astype(F32)
        for i in range(3):
            acc += got[(i, *at_index)].astype(F32)
        return acc.astype(BF)

    def around(i):
        return [lax.rem(k + i + 1, 4) for k in (z, y, x)]

    cuts2 = ((0, 3), (3, 3), (6, 2))
    cuts1 = ((0, 2), (2, 2), (4, 2))
    bufs2 = (r2, (pa2, pb2, pc2), (qa2, qb2, qc2), (ra2, rb2, rc2), g2, cuts2, 0)
    bufs1 = (r1, (pa1, pb1, pc1), (qa1, qb1, qc1), (ra1, rb1, rc1), g1, cuts1, 48)

    def start_first(i, bufs):
        recv, (pa, pb, pc), _, _, _, cuts, base = bufs
        sa, sb, sc = (pl.ds(*cut) for cut in cuts)
        zt = lax.rem(z + i + 1, 4)
        cps = []
        if i < 3:
            cps.append(send(recv.at[zt, :, :, sb], pb.at[i], rss, rrs, base + i, at(i + 1, 0, 0)))
        for k in range(3):
            _, yy, xx = around(k)
            cps.append(send(recv.at[zt, yy, :, sa], pa.at[k, zt], rss, rrs, base + 3 + 6 * i + k, at(0, k + 1, 0)))
            cps.append(send(recv.at[zt, :, xx, sc], pc.at[k, zt], rss, rrs, base + 6 + 6 * i + k, at(0, 0, 0, k + 1)))
        return cps

    def start_second(bufs):
        recv, (pa, pb, pc), (qa, qb, qc), _, _, cuts, base = bufs
        sa, sb, sc = (slice(a, a + n) for a, n in cuts)

        def one(k, carry):
            recv[k, y, :, sa] = total(recv[k, y, :, sa], pa, k)
            recv[z, k, :, sb] = total(recv[z, k, :, sb], pb, k)
            recv[k, :, x, sc] = total(recv[k, :, x, sc], pc, k)
            return carry

        lax.fori_loop(0, 4, one, 0)
        sa, sb, sc = (pl.ds(*cut) for cut in cuts)
        cps = []
        for i in range(3):
            zz, yy, _ = around(i)
            cps.append(send(recv.at[zz, y, :, sa], qa.at[i], rss, rrs, base + 27 + i, at(i + 1, 0, 0)))
            cps.append(send(recv.at[z, yy, :, sb], qb.at[i], rss, rrs, base + 30 + i, at(0, i + 1, 0)))
            cps.append(send(recv.at[:, yy, x, sc], qc.at[i], rss, rrs, base + 33 + i, at(0, i + 1, 0)))
        return cps

    def start_third(bufs):
        recv, _, (qa, qb, qc), (ra, rb, rc), _, cuts, base = bufs
        sa, sb, sc = (slice(a, a + n) for a, n in cuts)

        def one(k, carry):
            recv[z, y, k, sa] = total(recv[z, y, k, sa], qa, k)
            recv[z, y, k, sb] = total(recv[z, y, k, sb], qb, k)
            recv[k, y, x, sc] = total(recv[k, y, x, sc], qc, k)
            return carry

        lax.fori_loop(0, 4, one, 0)
        sa, sb, sc = (pl.ds(*cut) for cut in cuts)
        cps = []
        for i in range(3):
            zz, _, xx = around(i)
            cps.append(send(recv.at[z, y, xx, sa], ra.at[i], rss, rrs, base + 36 + i, at(0, 0, 0, i + 1)))
            cps.append(send(recv.at[z, y, xx, sb], rb.at[i], rss, rrs, base + 39 + i, at(0, 0, 0, i + 1)))
            cps.append(send(recv.at[zz, y, x, sc], rc.at[i], rss, rrs, base + 42 + i, at(i + 1, 0, 0)))
        return cps

    def start_last(bufs):
        recv, _, _, outs, gath, cuts, base = bufs
        for (a, n), got in zip(cuts, outs):
            gath[x, a : a + n] = total(recv[z, y, x, a : a + n], got)
        return [send(gath.at[x], gath.at[x], rss, rrs, base + 45 + i, at(0, 0, 0, i + 1)) for i in range(3)]

    two = []
    for i in range(4):
        piece(i, slice(0, B), d2, 64, r2, 0)
        if i:
            merge(i - 1, 8, r2, 0)
            two += start_first(i - 1, bufs2)
    for t in range(4):
        cols = slice(t * 256, (t + 1) * 256)
        back = dot_cols(d2[...], w2[H + t * 256 : H + (t + 1) * 256, :]).astype(BF)
        tmp[:, cols] = dot(adjt[...], back)
    merge(3, 8, r2, 0)
    two += start_first(3, bufs2)
    for t in range(4):
        cols = slice(t * 256, (t + 1) * 256)
        grad = tmp[:, cols] + dot_cols(d2[...], w2[cols, :])
        d1[:, cols] = (grad * pre1[:, cols]).astype(BF)
    one = []
    for i in range(4):
        piece(i, slice(B, 2 * B), d1, 48, r1, 4)
        if i:
            merge(i - 1, 6, r1, 4)
            one += start_first(i - 1, bufs1)
    merge(3, 6, r1, 4)
    one += start_first(3, bufs1)

    for cp in [ag[1]] + ag[3:] + fwd:
        cp.wait_recv()
    sub = lax.broadcasted_iota(jnp.int32, (256, 256), 0)

    def place(n, carry):
        for t in range(NODE // 256):
            cols = slice(t * 256, (t + 1) * 256)
            hit = sub + n * 256 == brow[0, t // 2 : t // 2 + 1, t % 2 * 256 : t % 2 * 256 + 256]
            sel[:, cols] = jnp.where(hit, 1.0, 0.0).astype(BF)
        slot = lax.rem(n, 2)
        out = pltpu.make_async_copy(
            stage.at[slot], hist_o.at[pl.ds(pl.multiple_of(n * 256, 256), 256)], osem.at[slot]
        )

        @pl.when(n >= 2)
        def _():
            out.wait()

        for t in range(4):
            cols = slice(t * 256, (t + 1) * 256)
            stage[slot, :, cols] = dot(sel[...], codes[:, cols]).astype(BF)
        out.start()
        return carry

    sc[...] = jnp.zeros((8, NODE), F32)
    lane_w = lax.broadcasted_iota(jnp.int32, (128, 128), 1)

    def place_scale(k, carry):
        rr, j = lax.div(k, 4), lax.rem(k, 4)
        col = idxc[pl.ds(pl.multiple_of(1024 + k * 128, 128), 128), :]
        val = jnp.broadcast_to(scmsg[rr, pl.ds(j, 1), :], (128, 128)).T
        for t in range(NODE // 128):
            got = jnp.where(col == lane_w + t * 128, val, 0.0)
            sc[:, t * 128 : (t + 1) * 128] += jnp.sum(got.reshape(16, 8, 128), axis=0)
        return carry

    wait(two)
    two += start_second(bufs2)
    lax.fori_loop(0, 4, place, 0)
    wait(two[27:])
    two += start_third(bufs2)
    wait(one)
    one += start_second(bufs1)
    lax.fori_loop(4, 7, place, 0)
    wait(two[36:])
    two += start_last(bufs2)
    wait(one[27:])
    one += start_third(bufs1)
    lax.fori_loop(7, 8, place, 0)
    lax.fori_loop(0, 16, place_scale, 0)
    out_sc = load(12, sc, sc_o)
    wait(one[36:])
    one += start_last(bufs1)
    for slot in range(2):
        pltpu.make_async_copy(stage.at[slot], hist_o.at[pl.ds(0, 256)], osem.at[slot]).wait()
    wait(two[45:])
    out_two = load(13, g2, two_o)
    wait(one[45:])
    out_one = load(0, g1, one_o)
    for cp in cps_h + ag + fwd + two + one:
        cp.wait_send()
    for cp in (out_sc, out_two, out_one):
        cp.wait()


def finish(hist_i, sc_i, two_i, one_i, hist_o, sc_o, g1_o, g2_o, room, sc, two, one, line, g1, g2, get, put):
    ins, outs = [], []
    for i in range(8):
        rows = pl.ds(i * 256, 256)
        ins.append(pltpu.make_async_copy(hist_i.at[rows], room.at[i], get.at[i]))
        outs.append(pltpu.make_async_copy(room.at[i], hist_o.at[rows], put.at[i]))
        ins[-1].start()
    small = ((sc_i, sc), (two_i, two), (one_i, one))
    ins_small = [pltpu.make_async_copy(src, dst, get.at[8 + i]) for i, (src, dst) in enumerate(small)]
    for came in ins_small:
        came.start()
    for came, gone in zip(ins, outs):
        came.wait()
        gone.start()
    for came in ins_small:
        came.wait()
    line[...] = jnp.sum(sc[...], axis=0).astype(BF)
    for src, dst, subs in ((two, g2, 8), (one, g1, 6)):
        for t in range(4):
            for k in range(subs):
                r0, c0 = k // 2 * 16, t * 256 + k % 2 * 128
                dst[r0 : r0 + 16, c0 : c0 + 128] = src[t, k].astype(F32)
    for i, (src, dst) in enumerate(((line, sc_o), (g1, g1_o), (g2, g2_o))):
        outs.append(pltpu.make_async_copy(src, dst, put.at[8 + i]))
        outs[-1].start()
    for gone in outs:
        gone.wait()


def shards(feat_codes, feat_scales, hist_codes, hist_scales, batch_rows, send_rows, send_counts,
           block_ids, block_counts, tiles, w_one, w_two, cotangent):
    hbm = pl.BlockSpec(memory_space=pl.ANY)
    smem = pl.BlockSpec(memory_space=pltpu.SMEM)
    v = pltpu.VMEM
    dma = pltpu.SemaphoreType.DMA
    def sums(na, nb, nc):
        tile = (16, 128)
        return [
            v((4, 4, 4, na + nb + nc, *tile), BF),
            v((3, 4, 4, na, *tile), BF), v((3, 4, 4, nb, *tile), BF), v((3, 4, 4, nc, *tile), BF),
            v((3, 4, na, *tile), BF), v((3, 4, nb, *tile), BF), v((3, 4, nc, *tile), BF),
            v((3, na, *tile), BF), v((3, nb, *tile), BF), v((3, nc, *tile), BF),
            v((4, na + nb + nc, *tile), BF),
        ]

    scratch = [
        v((1, 4, B), jnp.int32), v((1, 1, 32, 32), jnp.int32), v((1, 1, 32), jnp.int32), v((NODE,), BF), v((NODE,), BF),
        v((8, NODE), F32),
        v((NODE, H), BF), v((2 * F, H), BF), v((2 * H, H), BF), v((QB, KB, BLK, BLK), BF), v((B, H), BF),
        v((3072, 128), jnp.int32), v((B, NTAB * BLK), BF), v((B, B), BF), v((256, NODE), BF),
        v((16, 64, F), BF), v((16, 64, H), BF), v((1024, F), BF), v((1024, H), BF),
        v((B, 2 * F), BF), v((B, 2 * H), BF), v((B, H), F32), v((B, H), F32), v((B, H), F32),
        v((B, H), BF), v((B, H), BF), v((4 * B, H), BF), v((4, 8, 128), F32), v((2, 256, H), BF),
        v((4, 4, 2, 4, 8, 16, 128), BF), *sums(3, 3, 2), *sums(2, 2, 2),
        dma((14,)), dma((2,)), dma((31,)), dma((31,)), dma((31,)), dma((31,)),
        dma((9,)), dma((9,)), dma((8,)), dma((8,)), dma((96,)), dma((96,)),
    ]
    made = pl.pallas_call(
        kernel,
        out_shape=(
            jax.ShapeDtypeStruct((NODE, H), BF),
            jax.ShapeDtypeStruct((8, NODE), F32),
            jax.ShapeDtypeStruct((4, 8, 16, 128), BF),
            jax.ShapeDtypeStruct((4, 6, 16, 128), BF),
        ),
        in_specs=[smem] * 2 + [hbm] * 11,
        out_specs=(hbm,) * 4,
        scratch_shapes=scratch,
        compiler_params=pltpu.CompilerParams(
            collective_id=0, has_side_effects=True, vmem_limit_bytes=62 << 20
        ),
        cost_estimate=pl.CostEstimate(flops=30_000_000_000, bytes_accessed=30_000_000, transcendentals=1_000_000),
    )(
        block_ids, block_counts, batch_rows, send_rows, send_counts, feat_scales, hist_scales,
        feat_codes, hist_codes, tiles[0, 0], w_one, w_two, cotangent[0, 0],
    )
    return pl.pallas_call(
        finish,
        out_shape=(
            jax.ShapeDtypeStruct((NODE, H), BF),
            jax.ShapeDtypeStruct((NODE,), BF),
            jax.ShapeDtypeStruct((48, H), F32),
            jax.ShapeDtypeStruct((64, H), F32),
        ),
        in_specs=[hbm] * 4,
        out_specs=(hbm,) * 4,
        scratch_shapes=[
            v((8, 256, H), BF), v((8, NODE), F32), v((4, 8, 16, 128), BF), v((4, 6, 16, 128), BF),
            v((NODE,), BF), v((48, H), F32), v((64, H), F32), dma((11,)), dma((11,)),
        ],
        compiler_params=pltpu.CompilerParams(vmem_limit_bytes=60 << 20),
    )(*made)


def solution(mesh):
    in_specs = (
        P("owner", None), P("owner"), P("owner", None), P("owner"), P("owner", None, None),
        P("owner", "rep", None, None), P("owner", "rep", None), P("owner", "rep", None, None),
        P("owner", "rep", None), P("owner", "rep", None, None, None, None), P(), P(),
        P("owner", "rep", None, None),
    )
    out_specs = (P("owner", None), P("owner"), P("owner", None), P("owner", None))
    return jax.shard_map(shards, mesh=mesh, in_specs=in_specs, out_specs=out_specs, check_vma=False)
```

time: 125 us -> 104 us (0.83)
  local copies, waits for them, and re-layouts: 13.4 us -> 0 us
  other arithmetic: 4.07 us -> 0 us
  Pallas kernels: 106 us -> 103 us
    unnamed x9 -> x0, local copies, waits for them, and re-layouts: 8.08 us -> none
    pallas_call x1, Pallas kernels: 106 us -> 98.7 us  [shards(): pl.pallas_call(kernel, out_shape=(jax.ShapeDtypeStruct((NODE, H), BF), ja...]
    pallas_call x0 -> x1, Pallas kernels: none -> 3.93 us  [shards(): pl.pallas_call(finish, out_shape=(jax.ShapeDtypeStruct((NODE, H), BF), ja...]
    broadcast_in_dim x1 -> x0, local copies, waits for them, and re-layouts: 2.21 us -> none  [shards(): jnp.broadcast_to(jnp.concatenate([picks, placed])[:, None], (3072, 128))]
    squeeze x2 -> x0, local copies, waits for them, and re-layouts: 1.55 us -> none  [the longest x1 0.79 us: shards(): picks = jnp.where(live, send_rows[0, 0], -1).reshape(-1)]
    reduce_sum x1 -> x0, other arithmetic: 1.46 us -> none  [shards(): return (hist_out, jnp.sum(sc, axis=0).astype(BF), g1, g2)]
    lt x2 -> x0, other arithmetic: 1.46 us -> none  [the longest x1 0.73 us: shards(): live = jnp.arange(32)[None, :] < send_counts[0, 0][:, None]]
    another operation x2 -> x0, local copies, waits for them, and re-layouts: 1.39 us -> none  [shards(): scales = jnp.stack([feat_scales, hist_scales]).astype(F32)]
where the time goes in v1:
time: 104 us; the launch traced here: 103 us
  Pallas kernels  103 us (99%)
    pallas_call x1, Pallas kernels, shards(): pl.pallas_call(kernel, out_shape=(jax.ShapeDtypeStruct((NODE, H), BF), ja...  98.7 us
    pallas_call x1, Pallas kernels, shards(): pl.pallas_call(finish, out_shape=(jax.ShapeDtypeStruct((NODE, H), BF), ja...  3.93 us

profile of v1, /device:TPU:0, one launch (start us, length us, event | category | flops | bytes accessed | tf_op | source)
XLA Modules:
  0.0 103.4 jit_solution(15433028249014122047)
XLA Ops:
  0.6 98.7 %shard_map.156 = (bf16[2048,1024]{1,0:T(8,128)(2,1)}, f32[8,2048]{1,0:T(8,128)}, bf16[4,8,16,128]{3,2,1,0:T(8,128)(2,1)}, bf16[4,6,16,128]{3,2,1,0:T(8,128)(2,1)}) custom-call(s32[1,1,4,8]{3,2,1,0:T(4,128)} %ids.1, s32[1,1,4]{2,1,0:T(1,128)} %counts.1, s32[1,4,512]{2,1,0:T(4,128)} %brow_h.1, s32[1,1,32,32]{3,2,1,0:T(8,128)} %srow_h.1, s32[1,1,32]{2,1,0:T(1,128)} %scount_h.1, ...), custom_call_target="tpu_custom_call" | custom-call | flops 30000001024 | bytes 30000000 | tf_op jit(solution)/shard_map/pallas_call | solution.py:492
  99.3 3.9 %shard_map.157 = (bf16[2048,1024]{1,0:T(8,128)(2,1)}, bf16[2048]{0:T(1024)(128)(2,1)}, f32[48,1024]{1,0:T(8,128)}, f32[64,1024]{1,0:T(8,128)}) custom-call(bf16[2048,1024]{1,0:T(8,128)(2,1)} %get-tuple-element.8.hist_i, f32[8,2048]{1,0:T(8,128)} %get-tuple-element.9.sc_i, bf16[4,8,16,128]{3,2,1,0:T(8,128)(2,1)} %get-tuple-element.10.two_i, ...), custom_call_target="tpu_custom_call" | custom-call | tf_op jit(solution)/shard_map/pallas_call | solution.py:511

commit v2 on v1

--- a/solution.py
+++ b/solution.py
@@ -47,7 +47,7 @@
 def kernel(
     ids, counts, brow_h, srow_h, scount_h, fscale_h, hscale_h, feat_h, hist_h, tiles_h, w1_h, w2_h, cot_h,
     hist_o, sc_o, two_o, one_o,
-    brow, srow, scount, fscale, hscale, sc,
+    brow, srow, scount, fscale, hscale, sc, scol,
     table, w1, w2, tiles, cot, idxc, adj, adjt, sel, sendf, sendh, recvf, recvh,
     left1, left2, pre1, pre2, tmp, d2, d1, codes, scmsg, stage, part,
     r2, pa2, pb2, pc2, qa2, qb2, qc2, ra2, rb2, rc2, g2,
@@ -102,14 +102,10 @@
     for d in range(32):
         idxc[d * 32 : (d + 1) * 32, :] = jnp.broadcast_to(turned[:, d : d + 1], (32, 128))
 
-    def spread(k, carry):
-        line = brow[0, pl.ds(k, 1), :]
-        for j in range(4):
-            wide = jnp.broadcast_to(line[:, j * 128 : (j + 1) * 128], (128, 128)).T
-            idxc[pl.ds(pl.multiple_of(1024 + k * B + j * 128, 128), 128), :] = wide
-        return carry
-
-    lax.fori_loop(0, 4, spread, 0)
+    line = brow[0, pl.ds(x, 1), :]
+    for j in range(4):
+        wide = jnp.broadcast_to(line[:, j * 128 : (j + 1) * 128], (128, 128)).T
+        idxc[1024 + j * 128 : 1024 + (j + 1) * 128, :] = wide
     scales = (fscale[...].astype(F32).reshape(1, NODE), hscale[...].astype(F32).reshape(1, NODE))
 
     lane = lax.broadcasted_iota(jnp.int32, (64, 128), 1)
@@ -151,7 +147,7 @@
     for chips in ROUNDS:
         cps_f += halo(chips, F, 0, sendf, recvf, fss, frs, len(cps_f), [])
     for i in range(2):
-        pick([1024 + x * B + i * 256 + j * 64 for j in range(4)], 0)
+        pick([1024 + i * 256 + j * 64 for j in range(4)], 0)
         for t in range(F // 256):
             cols = slice(t * 256, (t + 1) * 256)
             left1[i * 256 : (i + 1) * 256, cols] = dot(sel[...], table[:, cols]).astype(BF)
@@ -170,42 +166,47 @@
 
     lax.fori_loop(0, QB, fill, 0)
     adjt[...] = adj[:, :B].T
+    ld_w1.wait()
+    for t in range(F // 256):
+        cols = slice(t * 256, (t + 1) * 256)
+        tmp[:, cols] = dot(adj[:, :B], left1[:, cols])
+    for t in range(4):
+        cols = slice(t * 256, (t + 1) * 256)
+        pre1[:, cols] = dot(left1[:, :F], w1[:F, cols])
     ld_hist.wait()
     cps_h = []
     for chips, (k0, k1) in zip(ROUNDS[:3], ((0, 16), (16, 23), (23, 31))):
         cps_h += halo(chips, H, 1, sendh, recvh, hss, hrs, len(cps_h), cps_f[k0:k1])
 
-    ld_w1.wait()
-    for t in range(F // 256):
-        cols = slice(t * 256, (t + 1) * 256)
-        tmp[:, cols] = dot(adj[:, :B], left1[:, cols])
-    for t in range(4):
-        cols = slice(t * 256, (t + 1) * 256)
-        pre1[:, cols] = dot(left1[:, :F], w1[:F, cols])
     for cp in cps_f:
         cp.wait_recv()
-    ag = []
-    for i in range(2):
-        rows = slice(i * 256, (i + 1) * 256)
+    ag, right, left = [], {}, {}
+
+    def pass_on(q, dx, group, k):
+        mine = pl.ds(pl.multiple_of(group * B + q * 128, 128), 128)
+        return send(codes.at[mine], codes.at[mine], ass, ars, k, at(0, 0, 0, dx))
+
+    for q in (0, 2, 1, 3):
+        rows = slice(q * 128, (q + 1) * 128)
         left1[rows, F:] = (tmp[rows, :F] + dot(adj[rows, B:], recvf[...])).astype(BF)
         pre = pre1[rows, :] + dot(left1[rows, F:], w1[F:, :])
         sig = jax.nn.sigmoid(pre)
         hid = (pre * sig).astype(BF)
-        pre1[rows, :] = swish_slope(pre, sig)
+        pre1[rows, :] = pre
         left2[rows, :H] = hid
         wide = hid.astype(F32)
         scale = (jnp.max(jnp.abs(wide), axis=1, keepdims=True) + 1e-5).astype(BF).astype(F32)
-        mine = pl.ds(pl.multiple_of(x * B + i * 256, 256), 256)
-        codes[mine, :] = (wide * (1.0 / scale)).astype(BF)
-        for j in range(2):
-            wide = jnp.broadcast_to(scale[j * 128 : (j + 1) * 128], (128, 128)).T
-            scmsg[x, 2 * i + j : 2 * i + j + 1, :] = wide[0:1]
-        ag.append(send(codes.at[mine], codes.at[mine], ass, ars, i, at(0, 0, 0, 1)))
-    for i in (1, 0):
-        mine = pl.ds(pl.multiple_of(x * B + i * 256, 256), 256)
-        ag.append(send(codes.at[mine], codes.at[mine], ass, ars, 2 + i, at(0, 0, 0, 3)))
+        codes[pl.ds(pl.multiple_of(x * B + q * 128, 128), 128), :] = (wide * (1.0 / scale)).astype(BF)
+        scmsg[x, q : q + 1, :] = jnp.broadcast_to(scale, (128, 128)).T[0:1]
+        if q < 2:
+            right[q] = pass_on(q, 1, x, q)
+        else:
+            left[q] = pass_on(q, 3, x, 4 + q)
+    for q in (0, 1):
+        right[2 + q] = pass_on(2 + q, 1, x, 2 + q)
+        left[q] = pass_on(q, 3, x, 4 + q)
     for dx in (1, 2, 3):
-        ag.append(send(scmsg.at[x], scmsg.at[x], ass, ars, 5 + dx, at(0, 0, 0, dx)))
+        ag.append(send(scmsg.at[x], scmsg.at[x], ass, ars, 11 + dx, at(0, 0, 0, dx)))
 
     cps_h += halo(ROUNDS[3], H, 1, sendh, recvh, hss, hrs, len(cps_h), [])
 
@@ -220,12 +221,18 @@
         cols = slice(t * 256, (t + 1) * 256)
         table[cols, B:] = left1[:, cols].T
 
-    ag[0].wait_recv()
-    far = pl.ds(pl.multiple_of(lax.rem(x + 3, 4) * B, B), 256)
-    fwd = [send(codes.at[far], codes.at[far], ass, ars, 4, at(0, 0, 0, 1))]
-    ag[2].wait_recv()
-    far = pl.ds(pl.multiple_of(lax.rem(x + 1, 4) * B + 256, 256), 256)
-    fwd.append(send(codes.at[far], codes.at[far], ass, ars, 5, at(0, 0, 0, 3)))
+    for t in range(4):
+        cols = slice(t * 256, (t + 1) * 256)
+        pre = pre1[:, cols]
+        pre1[:, cols] = swish_slope(pre, jax.nn.sigmoid(pre))
+
+    fwd = []
+    for q in (0, 1):
+        right[q].wait_recv()
+        fwd.append(pass_on(q, 1, lax.rem(x + 3, 4), 8 + q))
+    for q in (2, 3):
+        left[q].wait_recv()
+        fwd.append(pass_on(q, 3, lax.rem(x + 1, 4), 8 + q))
 
     for cp in cps_h:
         cp.wait_recv()
@@ -367,8 +374,11 @@
     merge(3, 6, r1, 4)
     one += start_first(3, bufs1)
 
-    for cp in [ag[1]] + ag[3:] + fwd:
+    for cp in [right[2], right[3], left[0], left[1]] + ag + fwd:
         cp.wait_recv()
+    for k in range(16):
+        line = scmsg[k // 4, k % 4 : k % 4 + 1, :]
+        scol[k * 128 : (k + 1) * 128, :] = jnp.broadcast_to(line, (128, 128)).T.astype(BF)
     sub = lax.broadcasted_iota(jnp.int32, (256, 256), 0)
 
     def place(n, carry):
@@ -389,44 +399,36 @@
             cols = slice(t * 256, (t + 1) * 256)
             stage[slot, :, cols] = dot(sel[...], codes[:, cols]).astype(BF)
         out.start()
+        col = dot(sel[...], scol[...])
+        for h in range(2):
+            lanes = pl.ds(pl.multiple_of(n * 256 + h * 128, 128), 128)
+            sc[:, lanes] = col[h * 128 : (h + 1) * 128].T[:8]
         return carry
 
-    sc[...] = jnp.zeros((8, NODE), F32)
-    lane_w = lax.broadcasted_iota(jnp.int32, (128, 128), 1)
-
-    def place_scale(k, carry):
-        rr, j = lax.div(k, 4), lax.rem(k, 4)
-        col = idxc[pl.ds(pl.multiple_of(1024 + k * 128, 128), 128), :]
-        val = jnp.broadcast_to(scmsg[rr, pl.ds(j, 1), :], (128, 128)).T
-        for t in range(NODE // 128):
-            got = jnp.where(col == lane_w + t * 128, val, 0.0)
-            sc[:, t * 128 : (t + 1) * 128] += jnp.sum(got.reshape(16, 8, 128), axis=0)
-        return carry
-
+    lax.fori_loop(0, 2, place, 0)
     wait(two)
     two += start_second(bufs2)
-    lax.fori_loop(0, 4, place, 0)
+    lax.fori_loop(2, 4, place, 0)
     wait(two[27:])
     two += start_third(bufs2)
     wait(one)
     one += start_second(bufs1)
-    lax.fori_loop(4, 7, place, 0)
+    lax.fori_loop(4, 6, place, 0)
     wait(two[36:])
     two += start_last(bufs2)
     wait(one[27:])
     one += start_third(bufs1)
-    lax.fori_loop(7, 8, place, 0)
-    lax.fori_loop(0, 16, place_scale, 0)
-    out_sc = load(12, sc, sc_o)
+    lax.fori_loop(6, 8, place, 0)
     wait(one[36:])
     one += start_last(bufs1)
     for slot in range(2):
         pltpu.make_async_copy(stage.at[slot], hist_o.at[pl.ds(0, 256)], osem.at[slot]).wait()
+    out_sc = load(12, sc, sc_o)
     wait(two[45:])
     out_two = load(13, g2, two_o)
     wait(one[45:])
     out_one = load(0, g1, one_o)
-    for cp in cps_h + ag + fwd + two + one:
+    for cp in cps_h + ag + list(right.values()) + list(left.values()) + fwd + two + one:
         cp.wait_send()
     for cp in (out_sc, out_two, out_one):
         cp.wait()
@@ -448,7 +450,7 @@
         gone.start()
     for came in ins_small:
         came.wait()
-    line[...] = jnp.sum(sc[...], axis=0).astype(BF)
+    line[...] = jnp.max(sc[...], axis=0).astype(BF)
     for src, dst, subs in ((two, g2, 8), (one, g1, 6)):
         for t in range(4):
             for k in range(subs):
@@ -479,15 +481,15 @@
 
     scratch = [
         v((1, 4, B), jnp.int32), v((1, 1, 32, 32), jnp.int32), v((1, 1, 32), jnp.int32), v((NODE,), BF), v((NODE,), BF),
-        v((8, NODE), F32),
+        v((8, NODE), F32), v((NODE, 128), BF),
         v((NODE, H), BF), v((2 * F, H), BF), v((2 * H, H), BF), v((QB, KB, BLK, BLK), BF), v((B, H), BF),
-        v((3072, 128), jnp.int32), v((B, NTAB * BLK), BF), v((B, B), BF), v((256, NODE), BF),
+        v((1536, 128), jnp.int32), v((B, NTAB * BLK), BF), v((B, B), BF), v((256, NODE), BF),
         v((16, 64, F), BF), v((16, 64, H), BF), v((1024, F), BF), v((1024, H), BF),
         v((B, 2 * F), BF), v((B, 2 * H), BF), v((B, H), F32), v((B, H), F32), v((B, H), F32),
         v((B, H), BF), v((B, H), BF), v((4 * B, H), BF), v((4, 8, 128), F32), v((2, 256, H), BF),
         v((4, 4, 2, 4, 8, 16, 128), BF), *sums(3, 3, 2), *sums(2, 2, 2),
         dma((14,)), dma((2,)), dma((31,)), dma((31,)), dma((31,)), dma((31,)),
-        dma((9,)), dma((9,)), dma((8,)), dma((8,)), dma((96,)), dma((96,)),
+        dma((15,)), dma((15,)), dma((8,)), dma((8,)), dma((96,)), dma((96,)),
     ]
     made = pl.pallas_call(
         kernel,

time: 104 us -> 103 us (level)
  no operation moved by 1% of the time
where the time goes in v2:
time: 103 us
  Pallas kernels  102 us (99%)
    pallas_call x1, Pallas kernels, shards(): pl.pallas_call(kernel, out_shape=(jax.ShapeDtypeStruct((NODE, H), BF), ja...  97.8 us
    pallas_call x1, Pallas kernels, shards(): pl.pallas_call(finish, out_shape=(jax.ShapeDtypeStruct((NODE, H), BF), ja...  3.93 us

profile of v2, /device:TPU:0, one launch (start us, length us, event | category | flops | bytes accessed | tf_op | source)
XLA Modules:
  0.0 102.6 jit_solution(4449183780239861746)
XLA Ops:
  0.6 97.8 %shard_map.156 = (bf16[2048,1024]{1,0:T(8,128)(2,1)}, f32[8,2048]{1,0:T(8,128)}, bf16[4,8,16,128]{3,2,1,0:T(8,128)(2,1)}, bf16[4,6,16,128]{3,2,1,0:T(8,128)(2,1)}) custom-call(s32[1,1,4,8]{3,2,1,0:T(4,128)} %ids.1, s32[1,1,4]{2,1,0:T(1,128)} %counts.1, s32[1,4,512]{2,1,0:T(4,128)} %brow_h.1, s32[1,1,32,32]{3,2,1,0:T(8,128)} %srow_h.1, s32[1,1,32]{2,1,0:T(1,128)} %scount_h.1, ...), custom_call_target="tpu_custom_call" | custom-call | flops 30000001024 | bytes 30000000 | tf_op jit(solution)/shard_map/pallas_call | solution.py:494
  98.5 3.9 %shard_map.157 = (bf16[2048,1024]{1,0:T(8,128)(2,1)}, bf16[2048]{0:T(1024)(128)(2,1)}, f32[48,1024]{1,0:T(8,128)}, f32[64,1024]{1,0:T(8,128)}) custom-call(bf16[2048,1024]{1,0:T(8,128)(2,1)} %get-tuple-element.8.hist_i, f32[8,2048]{1,0:T(8,128)} %get-tuple-element.9.sc_i, bf16[4,8,16,128]{3,2,1,0:T(8,128)(2,1)} %get-tuple-element.10.two_i, ...), custom_call_target="tpu_custom_call" | custom-call | tf_op jit(solution)/shard_map/pallas_call | solution.py:513
